TPU v7x, 256 devices: a whole 4x4x8 slice. The times are simulated.
256 devices in a mesh: row: 8 (over y, x_hi), col: 32 (over z, x_lo, core).
Axes of the slice: x: 4 (x_hi: 2, x_lo: 2; x = x_hi * 2 + x_lo), y: 4, z: 8, core: 2. Of those that a mesh axis runs over, the one named last changes fastest.
Arguments:
- reconstructor: bfloat16 [8192, 40960], P('row', 'col'), may hold values from -0.03125 to 0.03125
- slopes: bfloat16 [40960, 2048], P('col', 'row'), may hold values from -6 to 6
- commands: float32 [2048, 8192], P('col', 'row'), may hold values from -6 to 6
Outputs:
- gradient: float32 [8192, 40960], P('row', 'col')
- residual: float32 [2048, 8192], P('col', 'row')
All inputs are finite; a program needn't handle non-finite values.
Results may differ from a plain program's by a relative error of at most 0.0028.
Values may be sent and summed in bfloat16 or wider, within the bound.
A program may use at most 128 MiB of HBM per device.

v0:
```python
import jax
import jax.numpy as jnp
from jax import lax
from jax.sharding import PartitionSpec as P


def on_device(reconstructor, slopes, commands):
    slopes_all = lax.all_gather(slopes, "row", axis=1, tiled=True)
    frame_total = slopes_all.shape[1]
    residual = (
        lax.psum_scatter(
            lax.dot_general(
                slopes_all,
                reconstructor,
                (((0,), (1,)), ((), ())),
                preferred_element_type=jnp.float32,
            ),
            "col",
            scatter_dimension=0,
            tiled=True,
        )
        - commands
    )
    residual_low = residual.astype(jnp.bfloat16)
    residual_all = lax.all_gather(residual_low, "col", axis=0, tiled=True)
    summed_frames = lax.dot_general(
        residual_all, slopes_all, (((0,), (1,)), ((), ())), preferred_element_type=jnp.float32
    )
    scale_factor = 1.0 / jnp.sqrt(jnp.float32(frame_total))
    return (summed_frames * scale_factor, residual)


def solution(mesh):
    in_specs = (P("row", "col"), P("col", "row"), P("col", "row"))
    out_specs = (P("row", "col"), P("col", "row"))
    return jax.shard_map(
        on_device, mesh=mesh, in_specs=in_specs, out_specs=out_specs, check_vma=False
    )
```

profile of v0, /device:TPU:1, one launch (start us, length us, event | category | flops | bytes accessed | tf_op | source)
XLA Modules:
  0.0 327.0 jit_solution(12119461872882098629)
XLA Ops:
  7.2 0.0 copy-start
  7.2 0.0 all-gather.3.cloned.1.call-start
  7.2 0.7 all-gather.3.cloned.1.call-update
  7.9 0.0 reduce-scatter.2.cloned.1.call-start
  8.0 94.6 %all-gather.3.cloned.1.call-done = bf16[1280,2048]{1,0:T(8,128)(2,1)} async-done(((bf16[1280,256]{1,0:T(8,128)(2,1)}), bf16[1280,2048]{1,0:T(8,128)(2,1)}) %all-gather.3.cloned.1.call-update) | async-done | bytes 5242896 | tf_op jit(solution)/shard_map/all_gather | solution.py:8
  102.5 0.0 copy-done
  102.5 10.5 %fusion.1 = f32[2048,1024]{1,0:T(8,128)} fusion(bf16[1280,2048]{1,0:T(8,128)(2,1)} %all-gather.3.cloned.1.call-done, bf16[1024,1280]{1,0:T(8,128)(2,1)S(1)} %copy-done), kind=kOutput, calls=%fused_computation.2 | convolution fusion | flops 5368709120 | bytes 16252928 | tf_op jit(solution)/shard_map/dot_general | solution.py:12
  113.0 0.0 copy-start.1
  113.0 0.0 reduce-scatter.2.cloned.1.call-update
  113.0 0.0 all-gather.5.cloned.1.call-start
  113.1 125.2 %reduce-scatter.2.cloned.1.call-done = f32[64,1024]{1,0:T(8,128)} async-done(((f32[2048,1024]{1,0:T(8,128)}), f32[64,1024]{1,0:T(8,128)}) %reduce-scatter.2.cloned.1.call-update) | async-done | bytes 262160 | tf_op jit(solution)/shard_map/reduce_scatter | solution.py:11
  238.3 0.0 copy-done.1
  238.3 1.7 fusion
  240.0 0.0 all-gather.5.cloned.1.call-update
  240.0 70.0 %all-gather.5.cloned.1.call-done = bf16[2048,1024]{1,0:T(8,128)(2,1)} async-done(((bf16[64,1024]{1,0:T(8,128)(2,1)}), bf16[2048,1024]{1,0:T(8,128)(2,1)}) %all-gather.5.cloned.1.call-update) | async-done | bytes 4194320 | tf_op jit(solution)/shard_map/all_gather | solution.py:25
  310.0 10.5 %convolution_multiply_fusion = f32[1024,1280]{1,0:T(8,128)} fusion(bf16[2048,1024]{1,0:T(8,128)(2,1)} %all-gather.5.cloned.1.call-done, bf16[1280,2048]{1,0:T(8,128)(2,1)} %all-gather.3.cloned.1.call-done), kind=kOutput, calls=%fused_computation | convolution fusion | flops 5370019840 | bytes 14680064 | tf_op jit(solution)/shard_map/dot_general | solution.py:26
Async XLA Ops:
  7.2 95.4 %copy-start = (bf16[1024,1280]{1,0:T(8,128)(2,1)S(1)}, bf16[1024,1280]{1,0:T(8,128)(2,1)}, u32[]{:S(2)}) copy-start(bf16[1024,1280]{1,0:T(8,128)(2,1)} %param.3) | copy-start | bytes 7864324
  7.2 95.3 %all-gather.3.cloned.1.call-start = ((), (), s32[]{:S(2)}) async-start(), calls=%async_computation.1 | async-start | bytes 5898240 | tf_op jit(solution)/shard_map/all_gather | solution.py:8
  7.9 230.4 %reduce-scatter.2.cloned.1.call-start = ((), (), s32[]{:S(2)}) async-start(), calls=%async_computation.2 | async-start | bytes 8650752 | tf_op jit(solution)/shard_map/reduce_scatter | solution.py:11
  113.0 125.3 %copy-start.1 = (f32[64,1024]{1,0:T(8,128)S(1)}, f32[64,1024]{1,0:T(8,128)}, u32[]{:S(2)}) copy-start(f32[64,1024]{1,0:T(8,128)} %param.5) | copy-start | bytes 786436
  113.0 197.0 %all-gather.5.cloned.1.call-start = ((), (), s32[]{:S(2)}) async-start(), calls=%async_computation.3 | async-start | bytes 4325376 | tf_op jit(solution)/shard_map/all_gather | solution.py:25
Sparse Core Ops, SparseCore 0:
  10.5 91.9 all-gather.2
  113.1 125.0 reduce-scatter.1
  240.7 69.2 all-gather.4
where the time goes:
time: 327 us
  waiting for transfers between devices  290 us (89%)
  matrix products  21 us (6%)
  between operations  13.8 us (4%)
    reduce_scatter x1, waiting for transfers between devices, on_device(): lax.psum_scatter(lax.dot_general(slopes_all, reconstructor, (((0,), (1,))...  125 us
    all_gather x1, waiting for transfers between devices, on_device(): slopes_all = lax.all_gather(slopes, 'row', axis=1, tiled=True)  94.6 us
    all_gather x1, waiting for transfers between devices, on_device(): residual_all = lax.all_gather(residual_low, 'col', axis=0, tiled=True)  70 us
    dot_general x1, matrix products, on_device(): lax.dot_general(residual_all, slopes_all, (((0,), (1,)), ((), ())), prefe...  10.5 us
    dot_general x1, matrix products, on_device(): lax.dot_general(slopes_all, reconstructor, (((0,), (1,)), ((), ())), pref...  10.5 us
  transfers between devices with their start and end apart: 3, of which 3 were waited for; matrix products, arithmetic and copies ran while one was open for 0% of the time, Pallas kernels for 0%

commit v1 on v0

v1 whole, which is shorter than its diff:
```python
import functools

import jax
import jax.numpy as jnp
from jax import lax
from jax.experimental import pallas as pl
from jax.experimental.pallas import tpu as pltpu
from jax.sharding import PartitionSpec as P

MESH = pl.DeviceIdType.MESH

FULL = 1024
HALF = 512
SLICE = 64
DEPTH = 1280
BLOCK = 256
BLOCKS = 8
STAGES = 12
LEAD = 4


def code(v):
    return (v * jnp.abs(v) * (v * v)).astype(jnp.bfloat16)


def decode(b):
    b = b.astype(jnp.float32)
    m = jnp.maximum(jnp.abs(b), 1e-36)
    m = m * lax.rsqrt(m)
    m = m * lax.rsqrt(m)
    return jnp.where(b < 0, -m, m)


def kernel(
    r_hbm, s_hbm, c_hbm, g_ref, res_ref,
    r_ref, sall, cpad, cmd_t, acc, csend, crecv, zsend, zrecv, xsend, xrecv, rall, turned,
    in_sem, s_ss, s_rs, ss, rs,
):
    row, col = lax.axis_index("row"), lax.axis_index("col")
    y, xh = row // 2, row % 2
    z, xl, core = col // 4, (col // 2) % 2, col % 2
    quad = xl * 2 + core
    y_up = (((y + 1) % 4) * 2 + xh, col)
    y_dn = (((y + 3) % 4) * 2 + xh, col)
    x_far = (y * 2 + 1 - xh, col)
    z_up = (row, ((z + 1) % 8) * 4 + quad)
    z_dn = (row, ((z + 7) % 8) * 4 + quad)
    x_near = (row, z * 4 + (1 - xl) * 2 + core)
    twin = (row, z * 4 + xl * 2 + 1 - core)

    barrier = pltpu.get_barrier_semaphore()
    for device in (y_up, y_dn, x_far, z_up, z_dn, x_near, twin):
        pl.semaphore_signal(barrier, inc=1, device_id=device, device_id_type=MESH)

    s_in = pltpu.make_async_copy(s_hbm, sall.at[0], in_sem.at[0])
    r_in = pltpu.make_async_copy(r_hbm, r_ref, in_sem.at[1])
    s_in.start()
    r_in.start()
    cpad[...] = jnp.zeros_like(cpad)
    c_in = pltpu.make_async_copy(
        c_hbm, cpad.at[pl.ds(pl.multiple_of(quad * 64, 64), 64)], in_sem.at[2]
    )
    c_in.start()

    def remote(src, dst, send, recv, device):
        return pltpu.make_async_remote_copy(
            src_ref=src, dst_ref=dst, send_sem=send, recv_sem=recv,
            device_id=device, device_id_type=MESH,
        )

    mid = DEPTH // 2
    lo, hi = pl.ds(0, mid), pl.ds(mid, mid)
    s_moves = [
        remote(sall.at[0], sall.at[1], s_ss.at[0], s_rs.at[0], y_up),
        remote(sall.at[0], sall.at[2], s_ss.at[1], s_rs.at[1], y_dn),
        remote(sall.at[0], sall.at[3], s_ss.at[2], s_rs.at[2], x_far),
        remote(sall.at[1, lo], sall.at[4, lo], s_ss.at[3], s_rs.at[3], y_up),
        remote(sall.at[2, hi], sall.at[4, hi], s_ss.at[4], s_rs.at[4], y_dn),
        remote(sall.at[3], sall.at[5], s_ss.at[5], s_rs.at[5], y_up),
        remote(sall.at[3], sall.at[6], s_ss.at[6], s_rs.at[6], y_dn),
        remote(sall.at[4], sall.at[7], s_ss.at[7], s_rs.at[7], x_far),
    ]
    s_in.wait()
    pl.semaphore_wait(barrier, 7)
    for i in (0, 1, 2):
        s_moves[i].start()

    c_in.wait()
    cmd_t[...] = cpad[...].T
    g_ref[...] = jnp.zeros_like(g_ref)
    r_in.wait()

    dy = (z // 2 + 4 - y) % 4
    dx = (z % 2 + 2 - xh) % 2
    near = jnp.where(dy == 0, 0, jnp.where(dy == 3, 1, jnp.where(dy == 1, 2, 4)))
    far = jnp.where(dy == 0, 3, jnp.where(dy == 3, 5, jnp.where(dy == 1, 6, 7)))
    my_slot = jnp.where(dx == 0, near, far)

    own0 = core * HALF
    other0 = (1 - core) * HALF

    def rows(start, size):
        return pl.ds(pl.multiple_of(start, size), size)

    def part(at):
        return rows(((z + at + 8) % 8) * SLICE, SLICE)

    def full_part(at):
        return rows(own0 + ((z + at + 8) % 8) * SLICE, SLICE)

    def core_move(g):
        return remote(csend.at[g], crecv.at[g], ss.at[g, 0], rs.at[g, 0], twin)

    def up_move(g, i):
        return remote(zsend.at[g, i], zrecv.at[g, i], ss.at[g, 1 + i], rs.at[g, 1 + i], z_up)

    def dn_move(g, i):
        return remote(
            zsend.at[g, 4 + i], zrecv.at[g, 4 + i], ss.at[g, 5 + i], rs.at[g, 5 + i], z_dn
        )

    def x_move(g):
        return remote(xsend.at[g], xrecv.at[g], ss.at[g, 8], rs.at[g, 8], x_near)

    def out_up(g, i):
        here = rall.at[g, full_part(-i)]
        return remote(here, here, ss.at[g, 9 + i], rs.at[g, 9 + i], z_up)

    def in_up(g, i):
        here = rall.at[g, full_part(-i - 1)]
        return remote(here, here, ss.at[g, 9 + i], rs.at[g, 9 + i], z_up)

    def out_dn(g, i):
        here = rall.at[g, full_part(i)]
        return remote(here, here, ss.at[g, 12 + i], rs.at[g, 12 + i], z_dn)

    def in_dn(g, i):
        here = rall.at[g, full_part(i + 1)]
        return remote(here, here, ss.at[g, 12 + i], rs.at[g, 12 + i], z_dn)

    def out_core(g):
        here = rall.at[g, rows(own0, HALF)]
        return remote(here, here, ss.at[g, 16], rs.at[g, 16], twin)

    def in_core(g):
        here = rall.at[g, rows(other0, HALF)]
        return remote(here, here, ss.at[g, 16], rs.at[g, 16], twin)

    def both(g, at):
        return acc[g, part(at), :] + decode(crecv[g, part(at), :])

    def stage_predict(g):
        @pl.when(g == 1)
        def _():
            s_moves[0].wait_recv()
            s_moves[3].start()
            s_moves[1].wait_recv()
            s_moves[4].start()
            s_moves[2].wait_recv()
            s_moves[5].start()
            s_moves[6].start()

        @pl.when(g == 4)
        def _():
            s_moves[3].wait_recv()
            s_moves[4].wait_recv()
            s_moves[7].start()

        for slot in (5, 6, 7):

            @pl.when(g == slot)
            def _(slot=slot):
                s_moves[slot].wait_recv()

        mine = (g == my_slot).astype(jnp.float32)
        tile = 256

        def predicted(start):
            p = jnp.dot(
                r_ref[rows(start, tile), :], sall[g], preferred_element_type=jnp.float32
            )
            return p - cmd_t[rows(start, tile), :] * mine

        @pl.loop(0, HALF // tile)
        def _(i):
            csend[g, rows(i * tile, tile), :] = code(predicted(other0 + i * tile))

        core_move(g).start()

        @pl.loop(0, HALF // tile)
        def _(i):
            acc[g, rows(i * tile, tile), :] = predicted(own0 + i * tile)

    def stage_1(g):
        core_move(g).wait_recv()
        zsend[g, 0] = code(both(g, 4))
        up_move(g, 0).start()

    def stage_2(g):
        zsend[g, 4] = code(both(g, -3))
        dn_move(g, 0).start()
        up_move(g, 0).wait_recv()
        zsend[g, 1] = code(both(g, 3) + decode(zrecv[g, 0]))
        up_move(g, 1).start()

    def stage_3(g):
        dn_move(g, 0).wait_recv()
        zsend[g, 5] = code(both(g, -2) + decode(zrecv[g, 4]))
        dn_move(g, 1).start()
        up_move(g, 1).wait_recv()
        zsend[g, 2] = code(both(g, 2) + decode(zrecv[g, 1]))
        up_move(g, 2).start()

    def stage_4(g):
        dn_move(g, 1).wait_recv()
        zsend[g, 6] = code(both(g, -1) + decode(zrecv[g, 5]))
        dn_move(g, 2).start()
        up_move(g, 2).wait_recv()
        zsend[g, 3] = code(both(g, 1) + decode(zrecv[g, 2]))
        up_move(g, 3).start()

    def stage_5(g):
        dn_move(g, 2).wait_recv()
        up_move(g, 3).wait_recv()
        total = both(g, 0) + decode(zrecv[g, 6]) + decode(zrecv[g, 3])
        acc[g, part(0), :] = total
        xsend[g] = code(total)
        x_move(g).start()

    def stage_6(g):
        x_move(g).wait_recv()
        low = (acc[g, part(0), :] + decode(xrecv[g])).astype(jnp.bfloat16)
        rall[g, full_part(0), :] = low
        out_dn(g, 0).start()
        out_up(g, 0).start()

    def stage_7(g):
        in_dn(g, 0).wait_recv()
        out_dn(g, 1).start()
        in_up(g, 0).wait_recv()
        out_up(g, 1).start()

    def stage_8(g):
        in_dn(g, 1).wait_recv()
        out_dn(g, 2).start()
        in_up(g, 1).wait_recv()
        out_up(g, 2).start()

    def stage_9(g):
        in_dn(g, 2).wait_recv()
        out_dn(g, 3).start()
        in_up(g, 2).wait_recv()

    def stage_10(g):
        in_dn(g, 3).wait_recv()
        out_core(g).start()

    def stage_gradient(g):
        in_core(g).wait_recv()
        tile = 256

        @pl.loop(0, FULL // tile)
        def _(i):
            g_ref[rows(i * tile, tile), :] += lax.dot_general(
                rall[g, rows(i * tile, tile), :], sall[g],
                (((1,), (1,)), ((), ())), preferred_element_type=jnp.float32,
            )

        @pl.when(g == my_slot)
        def _():
            half = rall[g, :, pl.ds(pl.multiple_of(xl * 128, 128), 128)]
            turned[...] = half.astype(jnp.float32).T
            res_ref[...] = turned[rows(core * 64, 64), :]

        core_move(g).wait_send()
        for i in range(4):
            up_move(g, i).wait_send()
            out_dn(g, i).wait_send()
        for i in range(3):
            dn_move(g, i).wait_send()
            out_up(g, i).wait_send()
        x_move(g).wait_send()
        out_core(g).wait_send()

    stages = [
        stage_predict, stage_1, stage_2, stage_3, stage_4, stage_5, stage_6,
        stage_7, stage_8, stage_9, stage_10, stage_gradient,
    ]
    order = [10, 9, 8, 7, 6, 5, 4, 3, 2, 1, 0, 11]

    def tick(t, carry):
        for k in order:
            u = t - k
            g = jnp.where(u <= 0, 0, u - LEAD)
            active = (u == 0) | ((u > LEAD) & (u < BLOCKS + LEAD))

            @pl.when(active)
            def _(k=k, g=g):
                stages[k](g)

        return carry

    lax.fori_loop(0, BLOCKS + LEAD + STAGES - 1, tick, 0)
    for move in s_moves:
        move.wait_send()


def on_device(reconstructor, slopes, commands):
    vmem = pltpu.VMEM
    gradient, residual = pl.pallas_call(
        kernel,
        out_shape=(
            jax.ShapeDtypeStruct((FULL, DEPTH), jnp.float32),
            jax.ShapeDtypeStruct((64, FULL), jnp.float32),
        ),
        in_specs=[pl.BlockSpec(memory_space=pl.ANY)] * 3,
        out_specs=[pl.BlockSpec(memory_space=pltpu.VMEM)] * 2,
        scratch_shapes=[
            vmem((FULL, DEPTH), jnp.bfloat16),
            vmem((BLOCKS, DEPTH, BLOCK), jnp.bfloat16),
            vmem((BLOCK, FULL), jnp.float32),
            vmem((FULL, BLOCK), jnp.float32),
            vmem((BLOCKS, HALF, BLOCK), jnp.float32),
            vmem((BLOCKS, HALF, BLOCK), jnp.bfloat16),
            vmem((BLOCKS, HALF, BLOCK), jnp.bfloat16),
            vmem((BLOCKS, 7, SLICE, BLOCK), jnp.bfloat16),
            vmem((BLOCKS, 7, SLICE, BLOCK), jnp.bfloat16),
            vmem((BLOCKS, SLICE, BLOCK), jnp.bfloat16),
            vmem((BLOCKS, SLICE, BLOCK), jnp.bfloat16),
            vmem((BLOCKS, FULL, BLOCK), jnp.bfloat16),
            vmem((128, FULL), jnp.float32),
            pltpu.SemaphoreType.DMA((3,)),
            pltpu.SemaphoreType.DMA((8,)),
            pltpu.SemaphoreType.DMA((8,)),
            pltpu.SemaphoreType.DMA((BLOCKS, 17)),
            pltpu.SemaphoreType.DMA((BLOCKS, 17)),
        ],
        compiler_params=pltpu.CompilerParams(
            collective_id=0, has_side_effects=True, vmem_limit_bytes=56 << 20
        ),
        cost_estimate=pl.CostEstimate(
            flops=4 * 2048 * FULL * DEPTH, bytes_accessed=9 << 20, transcendentals=0
        ),
    )(reconstructor, slopes, commands)
    scale_factor = 1.0 / jnp.sqrt(jnp.float32(2048))
    return gradient * scale_factor, residual


def solution(mesh):
    in_specs = (P("row", "col"), P("col", "row"), P("col", "row"))
    out_specs = (P("row", "col"), P("col", "row"))
    return jax.shard_map(
        on_device, mesh=mesh, in_specs=in_specs, out_specs=out_specs, check_vma=False
    )
```

time: 327 us -> 106 us (0.32)
  waiting for transfers between devices: 290 us -> 0 us
  Pallas kernels: 0 us -> 99.3 us
  matrix products: 21 us -> 0 us
  between operations: 13.8 us -> 0.65 us
  other arithmetic: 1.72 us -> 5.34 us
    all_gather x2 -> x0, waiting for transfers between devices: 165 us -> none  [the longest x1 94.6 us: on_device(): slopes_all = lax.all_gather(slopes, 'row', axis=1, tiled=True)]
    reduce_scatter x1 -> x0, waiting for transfers between devices: 125 us -> none  [on_device(): lax.psum_scatter(lax.dot_general(slopes_all, reconstructor, (((0,), (1,))...]
    pallas_call x0 -> x1, Pallas kernels: none -> 99.3 us  [on_device(): pl.pallas_call(kernel, out_shape=(jax.ShapeDtypeStruct((FULL, DEPTH), jnp...]
    dot_general x2 -> x0, matrix products: 21 us -> none  [the longest x1 10.5 us: on_device(): lax.dot_general(residual_all, slopes_all, (((0,), (1,)), ((), ())), prefe...]
    mul x0 -> x1, other arithmetic: none -> 5.34 us  [on_device(): return (gradient * scale_factor, residual)]
  transfers between devices with their start and end apart: 3 -> 0, of which waited for: 3 -> 0; matrix products, arithmetic and copies ran while one was open for 0% -> 0% of each run, Pallas kernels for 0% -> 0%
where the time goes in v1:
time: 106 us
  Pallas kernels  99.3 us (94%)
  other arithmetic  5.34 us (5%)
    pallas_call x1, Pallas kernels, on_device(): pl.pallas_call(kernel, out_shape=(jax.ShapeDtypeStruct((FULL, DEPTH), jnp...  99.3 us
    mul x1, other arithmetic, on_device(): return (gradient * scale_factor, residual)  5.34 us

profile of v1, /device:TPU:1, one launch (start us, length us, event | category | flops | bytes accessed | tf_op | source)
XLA Modules:
  0.0 106.0 jit_solution(16240175641453951907)
XLA Ops:
  0.6 99.3 %shard_map.50 = (f32[1024,1280]{1,0:T(8,128)}, f32[64,1024]{1,0:T(8,128)}) custom-call(bf16[1024,1280]{1,0:T(8,128)(2,1)} %r_hbm.1, bf16[1280,256]{1,0:T(8,128)(2,1)} %s_hbm.1, f32[64,1024]{1,0:T(8,128)} %c_hbm.1), custom_call_target="tpu_custom_call" | custom-call | flops 10737418240 | bytes 9437184 | tf_op jit(solution)/shard_map/pallas_call | solution.py:310
  99.9 0.0 copy-start
  99.9 5.3 %broadcast_multiply_fusion = f32[1024,1280]{1,0:T(8,128)} fusion(f32[1024,1280]{1,0:T(8,128)} %get-tuple-element.4), kind=kLoop, calls=%fused_computation | loop fusion | flops 1310720 | bytes 10485760 | tf_op jit(solution)/shard_map/mul | solution.py:346
  105.2 0.0 copy-done
  105.2 0.7 copy.6
Async XLA Ops:
  99.9 5.3 %copy-start = (f32[64,1024]{1,0:T(8,128)S(1)}, f32[64,1024]{1,0:T(8,128)}, u32[]{:S(2)}) copy-start(f32[64,1024]{1,0:T(8,128)} %get-tuple-element.9) | copy-start | bytes 786436

commit v2 on v1

v2 whole, which is shorter than its diff:
```python
import functools

import jax
import jax.numpy as jnp
from jax import lax
from jax.experimental import pallas as pl
from jax.experimental.pallas import tpu as pltpu
from jax.sharding import PartitionSpec as P

MESH = pl.DeviceIdType.MESH

FULL = 1024
HALF = 512
SLICE = 64
DEPTH = 1280
BLOCK = 256
BLOCKS = 8
WHEN = (
    (0, 3, 6, 10, 15, 18, 21, 24),
    (1, 4, 8, 11, 16, 20, 22, 25),
    (2, 7, 17, 18, 19, 23, 26, 30),
    (5, 12, 19, 21, 29, 28, 32, 34),
    (8, 18, 23, 24, 31, 32, 33, 35),
    (13, 20, 29, 30, 35, 36, 37, 39),
    (20, 27, 38, 34, 39, 40, 41, 42),
    (20, 27, 38, 36, 39, 41, 42, 43),
)
SEND_ON = (3, 6, 9, 10, 14, 15)


def code(v):
    return (v * jnp.abs(v) * (v * v)).astype(jnp.bfloat16)


def decode(b):
    b = b.astype(jnp.float32)
    m = jnp.maximum(jnp.abs(b), 1e-36)
    m = m * lax.rsqrt(m)
    m = m * lax.rsqrt(m)
    return jnp.where(b < 0, -m, m)


def kernel(
    r_hbm, s_hbm, c_hbm, g_ref, res_ref,
    r_ref, sall, cpad, cmd_t, acc, csend, crecv, near_s, near_r, far_s, far_r, sum_s, sum_r,
    xsend, xrecv, rall, turned,
    in_sem, s_ss, s_rs, ss, rs,
):
    row, col = lax.axis_index("row"), lax.axis_index("col")
    y, xh = row // 2, row % 2
    z, xl, core = col // 4, (col // 2) % 2, col % 2
    quad = xl * 2 + core
    y_up = (((y + 1) % 4) * 2 + xh, col)
    y_dn = (((y + 3) % 4) * 2 + xh, col)
    x_far = (y * 2 + 1 - xh, col)
    z_up = (row, ((z + 1) % 8) * 4 + quad)
    z_dn = (row, ((z + 7) % 8) * 4 + quad)
    z_up2 = (row, ((z + 2) % 8) * 4 + quad)
    z_dn2 = (row, ((z + 6) % 8) * 4 + quad)
    x_near = (row, z * 4 + (1 - xl) * 2 + core)
    twin = (row, z * 4 + xl * 2 + 1 - core)

    barrier = pltpu.get_barrier_semaphore()
    for device in (y_up, y_dn, x_far, z_up, z_dn, z_up2, z_dn2, x_near, twin):
        pl.semaphore_signal(barrier, inc=1, device_id=device, device_id_type=MESH)

    s_in = pltpu.make_async_copy(s_hbm, sall.at[0], in_sem.at[0])
    r_in = pltpu.make_async_copy(r_hbm, r_ref, in_sem.at[1])
    s_in.start()
    r_in.start()
    cpad[...] = jnp.zeros_like(cpad)
    def remote(src, dst, send, recv, device):
        return pltpu.make_async_remote_copy(
            src_ref=src, dst_ref=dst, send_sem=send, recv_sem=recv,
            device_id=device, device_id_type=MESH,
        )

    mid = DEPTH // 2
    lo, hi, every = pl.ds(0, mid), pl.ds(mid, mid), pl.ds(0, DEPTH)
    left, right = pl.ds(0, 128), pl.ds(128, 128)
    s_moves = [
        remote(sall.at[i, r0, c0], sall.at[j, r0, c1], s_ss.at[n], s_rs.at[n], device)
        for n, (i, j, r0, c0, c1, device) in enumerate((
            (0, 1, every, left, left, y_up),
            (0, 1, every, left, right, y_dn),
            (0, 2, every, right, left, y_up),
            (0, 2, every, right, right, y_dn),
            (0, 3, every, left, left, x_far),
            (0, 3, every, right, right, x_far),
            (1, 4, lo, left, left, y_up),
            (1, 4, hi, right, left, y_dn),
            (2, 4, lo, left, right, y_up),
            (2, 4, hi, right, right, y_dn),
            (3, 5, every, left, left, y_up),
            (3, 5, every, left, right, y_dn),
            (3, 6, every, right, left, y_up),
            (3, 6, every, right, right, y_dn),
            (4, 7, every, left, left, x_far),
            (4, 7, every, right, right, x_far),
        ))
    ]
    passes = [
        ((0, 1), (6, 7)), ((2, 3), (8, 9)), ((4,), (10, 11)), ((5,), (12, 13)), ((6, 7), (14,)),
        ((8, 9), (15,)),
    ]
    dy = (z // 2 + 4 - y) % 4
    dx = (z % 2 + 2 - xh) % 2
    beside = (dy == 1) | (dy == 3)
    my_slot = jnp.where(beside, 1 + 4 * dx + xl, jnp.where(dy == 0, 3 * dx, 4 + 3 * dx))
    my_half = jnp.where(beside, (dy == 1).astype(jnp.int32), xl)
    c_in = pltpu.make_async_copy(
        c_hbm,
        cpad.at[pl.ds(pl.multiple_of(my_half * 128 + core * 64, 64), 64)],
        in_sem.at[2],
    )
    c_in.start()
    s_in.wait()
    pl.semaphore_wait(barrier, 9)
    for i in (0, 1, 4, 2, 3, 5):
        s_moves[i].start()

    c_in.wait()
    cmd_t[...] = cpad[...].T
    g_ref[...] = jnp.zeros_like(g_ref)
    r_in.wait()

    own0 = core * HALF
    other0 = (1 - core) * HALF

    def rows(start, size):
        return pl.ds(pl.multiple_of(start, size), size)

    def part(at, size=SLICE, skip=0):
        return rows(((z + at + 8) % 8) * SLICE + skip, size)

    def full_part(at, size=SLICE, skip=0):
        return rows(own0 + ((z + at + 8) % 8) * SLICE + skip, size)

    def core_move(g):
        return remote(csend.at[g], crecv.at[g], ss.at[g, 0], rs.at[g, 0], twin)

    one, two = (z_up, z_dn), (z_up2, z_dn2)

    def near_move(g, d):
        return remote(near_s.at[g, d], near_r.at[g, d], ss.at[g, 1 + d], rs.at[g, 1 + d], one[d])

    def far_move(g, d):
        return remote(far_s.at[g, d], far_r.at[g, d], ss.at[g, 3 + d], rs.at[g, 3 + d], two[d])

    def sum_move(g, d):
        return remote(sum_s.at[g, d], sum_r.at[g, d], ss.at[g, 5 + d], rs.at[g, 5 + d], two[d])

    def x_move(g):
        return remote(xsend.at[g], xrecv.at[g], ss.at[g, 7], rs.at[g, 7], x_near)

    def spread(g, d, n, at, device, size=SLICE, skip=0):
        here = rall.at[g, full_part(at, size, skip)]
        return remote(here, here, ss.at[g, n + d], rs.at[g, n + d], device)

    def out_1(g, d):
        return spread(g, d, 8, 0, one[d])

    def in_1(g, d):
        return spread(g, d, 8, (-1, 1)[d], one[d])

    def out_2(g, d):
        return spread(g, d, 10, 0, two[d])

    def in_2(g, d):
        return spread(g, d, 10, (-2, 2)[d], two[d])

    def out_3(g, d):
        return spread(g, d, 12, (-2, 2)[d], one[d])

    def in_3(g, d):
        return spread(g, d, 12, (-3, 3)[d], one[d])

    def out_4(g, d):
        return spread(g, d, 14, (-2, 2)[d], two[d], SLICE // 2, d * SLICE // 2)

    def in_4(g, d):
        return spread(g, d, 14, 4, two[d], SLICE // 2, d * SLICE // 2)

    def out_core(g):
        here = rall.at[g, rows(own0, HALF)]
        return remote(here, here, ss.at[g, 16], rs.at[g, 16], twin)

    def in_core(g):
        here = rall.at[g, rows(other0, HALF)]
        return remote(here, here, ss.at[g, 16], rs.at[g, 16], twin)

    def both(g, at, size=SLICE, skip=0):
        here = part(at, size, skip)
        return acc[g, here, :] + decode(crecv[g, here, :])

    def pass_on(n):
        arrived, onward = passes[n]
        for i in arrived:
            s_moves[i].wait_recv()
        for i in onward:
            s_moves[i].start()

    def stage_predict(g):
        for slot in (5, 6, 7):

            @pl.when(g == slot)
            def _(slot=slot):
                s_moves[2 * slot].wait_recv()
                s_moves[2 * slot + 1].wait_recv()

        mine = (g == my_slot).astype(jnp.float32)
        tile = 512

        def predicted(start):
            p = jnp.dot(
                r_ref[rows(start, tile), :], sall[g], preferred_element_type=jnp.float32
            )
            return p - cmd_t[rows(start, tile), :] * mine

        @pl.loop(0, HALF // tile)
        def _(i):
            csend[g, rows(i * tile, tile), :] = code(predicted(other0 + i * tile))

        core_move(g).start()

        @pl.loop(0, HALF // tile)
        def _(i):
            acc[g, rows(i * tile, tile), :] = predicted(own0 + i * tile)

    half = SLICE // 2
    first, second = pl.ds(0, SLICE), pl.ds(SLICE, SLICE)

    def stage_1(g):
        core_move(g).wait_recv()
        for d, sign in ((0, 1), (1, -1)):
            far_s[g, d] = code(both(g, 4, half, d * half))
            far_move(g, d).start()
            near_s[g, d, second, :] = code(both(g, 3 * sign))
            near_s[g, d, first, :] = code(both(g, sign))
            near_move(g, d).start()

    def stage_2(g):
        for d, sign in ((0, 1), (1, -1)):
            near_move(g, d).wait_recv()
            far_move(g, d).wait_recv()
            for h in (0, 1):
                total = both(g, 2 * sign, half, h * half) + decode(
                    near_r[g, d, pl.ds(SLICE + h * half, half), :]
                )
                if h == d:
                    total = total + decode(far_r[g, d])
                sum_s[g, d, pl.ds(h * half, half), :] = code(total)
            sum_move(g, d).start()

    def stage_3(g):
        total = both(g, 0) + decode(near_r[g, 0, first, :]) + decode(near_r[g, 1, first, :])
        for d in (0, 1):
            sum_move(g, d).wait_recv()
            total = total + decode(sum_r[g, d])
        acc[g, part(0), :] = total
        xsend[g] = code(total)
        x_move(g).start()

    def stage_4(g):
        x_move(g).wait_recv()
        low = (acc[g, part(0), :] + decode(xrecv[g])).astype(jnp.bfloat16)
        rall[g, full_part(0), :] = low
        for d in (0, 1):
            out_2(g, d).start()
        for d in (0, 1):
            out_1(g, d).start()

    def stage_5(g):
        for d in (0, 1):
            in_2(g, d).wait_recv()
            out_4(g, d).start()
            out_3(g, d).start()

    def add_gradient(g, start):
        here = rows(start, HALF)
        g_ref[here, :] += lax.dot_general(
            rall[g, here, :], sall[g], (((1,), (1,)), ((), ())),
            preferred_element_type=jnp.float32,
        )

    def stage_6(g):
        for d in (0, 1):
            in_1(g, d).wait_recv()
            in_3(g, d).wait_recv()
            in_4(g, d).wait_recv()
        out_core(g).start()
        add_gradient(g, own0)

    def stage_gradient(g):
        in_core(g).wait_recv()
        add_gradient(g, other0)

        @pl.when(g == my_slot)
        def _():
            half = rall[g, :, pl.ds(pl.multiple_of(my_half * 128, 128), 128)]
            turned[...] = half.astype(jnp.float32).T
            res_ref[...] = turned[rows(core * 64, 64), :]

        core_move(g).wait_send()
        for move in (near_move, far_move, sum_move, out_1, out_2, out_3, out_4):
            for d in (0, 1):
                move(g, d).wait_send()
        x_move(g).wait_send()
        out_core(g).wait_send()

    stages = [
        stage_predict, stage_1, stage_2, stage_3, stage_4, stage_5, stage_6, stage_gradient,
    ]
    order = [6, 5, 4, 3, 2, 1, 0, 7]

    def tick(t, carry):
        for n, at in enumerate(SEND_ON):
            pl.when(t == at)(functools.partial(pass_on, n))
        for k in order:
            g, active = jnp.int32(0), t == WHEN[k][0]
            for i in range(1, BLOCKS):
                g = jnp.where(t == WHEN[k][i], i, g)
                active = active | (t == WHEN[k][i])

            @pl.when(active)
            def _(k=k, g=g):
                stages[k](g)

        return carry

    lax.fori_loop(0, max(WHEN[-1]) + 1, tick, 0)
    for move in s_moves:
        move.wait_send()


def on_device(reconstructor, slopes, commands):
    vmem = pltpu.VMEM
    gradient, residual = pl.pallas_call(
        kernel,
        out_shape=(
            pltpu.VMEM((FULL, DEPTH), jnp.float32),
            pltpu.VMEM((64, FULL), jnp.float32),
        ),
        in_specs=[pl.BlockSpec(memory_space=pl.ANY)] * 3,
        out_specs=[pl.BlockSpec(memory_space=pltpu.VMEM)] * 2,
        scratch_shapes=[
            vmem((FULL, DEPTH), jnp.bfloat16),
            vmem((BLOCKS, DEPTH, BLOCK), jnp.bfloat16),
            vmem((BLOCK, FULL), jnp.float32),
            vmem((FULL, BLOCK), jnp.float32),
            vmem((BLOCKS, HALF, BLOCK), jnp.float32),
            vmem((BLOCKS, HALF, BLOCK), jnp.bfloat16),
            vmem((BLOCKS, HALF, BLOCK), jnp.bfloat16),
            vmem((BLOCKS, 2, 2 * SLICE, BLOCK), jnp.bfloat16),
            vmem((BLOCKS, 2, 2 * SLICE, BLOCK), jnp.bfloat16),
            vmem((BLOCKS, 2, SLICE // 2, BLOCK), jnp.bfloat16),
            vmem((BLOCKS, 2, SLICE // 2, BLOCK), jnp.bfloat16),
            vmem((BLOCKS, 2, SLICE, BLOCK), jnp.bfloat16),
            vmem((BLOCKS, 2, SLICE, BLOCK), jnp.bfloat16),
            vmem((BLOCKS, SLICE, BLOCK), jnp.bfloat16),
            vmem((BLOCKS, SLICE, BLOCK), jnp.bfloat16),
            vmem((BLOCKS, FULL, BLOCK), jnp.bfloat16),
            vmem((128, FULL), jnp.float32),
            pltpu.SemaphoreType.DMA((3,)),
            pltpu.SemaphoreType.DMA((16,)),
            pltpu.SemaphoreType.DMA((16,)),
            pltpu.SemaphoreType.DMA((BLOCKS, 17)),
            pltpu.SemaphoreType.DMA((BLOCKS, 17)),
        ],
        compiler_params=pltpu.CompilerParams(
            collective_id=0, has_side_effects=True, vmem_limit_bytes=56 << 20
        ),
        cost_estimate=pl.CostEstimate(
            flops=4 * 2048 * FULL * DEPTH, bytes_accessed=9 << 20, transcendentals=0
        ),
    )(reconstructor, slopes, commands)
    scale_factor = 1.0 / jnp.sqrt(jnp.float32(2048))
    return gradient * scale_factor, residual


def solution(mesh):
    in_specs = (P("row", "col"), P("col", "row"), P("col", "row"))
    out_specs = (P("row", "col"), P("col", "row"))
    return jax.shard_map(
        on_device, mesh=mesh, in_specs=in_specs, out_specs=out_specs, check_vma=False
    )
```

time: 106 us -> 91.1 us (0.86)
  Pallas kernels: 99.3 us -> 86.8 us
  other arithmetic: 5.34 us -> 2.86 us
    pallas_call x1, Pallas kernels: 99.3 us -> 86.8 us  [on_device(): pl.pallas_call(kernel, out_shape=(pltpu.VMEM((FULL, DEPTH), jnp.float32),...]
    mul x1, other arithmetic: 5.34 us -> 2.86 us  [on_device(): return (gradient * scale_factor, residual)]
where the time goes in v2:
time: 91.1 us; the launch traced here: 91 us
  Pallas kernels  86.8 us (95%)
  other arithmetic  2.86 us (3%)
    pallas_call x1, Pallas kernels, on_device(): pl.pallas_call(kernel, out_shape=(pltpu.VMEM((FULL, DEPTH), jnp.float32),...  86.8 us
    mul x1, other arithmetic, on_device(): return (gradient * scale_factor, residual)  2.86 us

profile of v2, /device:TPU:1, one launch (start us, length us, event | category | flops | bytes accessed | tf_op | source)
XLA Modules:
  0.0 91.0 jit_solution(2394996339760305344)
XLA Ops:
  0.6 86.8 %shard_map.50 = (f32[1024,1280]{1,0:T(8,128)S(1)}, f32[64,1024]{1,0:T(8,128)S(1)}) custom-call(bf16[1024,1280]{1,0:T(8,128)(2,1)} %r_hbm.1, bf16[1280,256]{1,0:T(8,128)(2,1)} %s_hbm.1, f32[64,1024]{1,0:T(8,128)} %c_hbm.1), custom_call_target="tpu_custom_call" | custom-call | flops 10737418240 | bytes 9437184 | tf_op jit(solution)/shard_map/pallas_call | solution.py:338
  87.4 2.9 %broadcast_multiply_fusion = f32[1024,1280]{1,0:T(8,128)} fusion(f32[1024,1280]{1,0:T(8,128)S(1)} %get-tuple-element.4), kind=kLoop, calls=%fused_computation | loop fusion | flops 1310720 | bytes 10485760 | tf_op jit(solution)/shard_map/mul | solution.py:378
  90.3 0.7 copy.6

commit v3 on v2

--- a/solution.py
+++ b/solution.py
@@ -15,17 +15,18 @@
 DEPTH = 1280
 BLOCK = 256
 BLOCKS = 8
+PIECES = 8
 WHEN = (
-    (0, 3, 6, 10, 15, 18, 21, 24),
-    (1, 4, 8, 11, 16, 20, 22, 25),
-    (2, 7, 17, 18, 19, 23, 26, 30),
-    (5, 12, 19, 21, 29, 28, 32, 34),
-    (8, 18, 23, 24, 31, 32, 33, 35),
-    (13, 20, 29, 30, 35, 36, 37, 39),
-    (20, 27, 38, 34, 39, 40, 41, 42),
-    (20, 27, 38, 36, 39, 41, 42, 43),
+    (0, 3, 5, 8, 11, 14, 16, 19),
+    (1, 4, 8, 9, 12, 15, 17, 20),
+    (2, 7, 12, 13, 15, 19, 21, 23),
+    (4, 10, 22, 16, 18, 24, 25, 30),
+    (5, 14, 23, 19, 22, 28, 27, 31),
+    (9, 17, 30, 23, 26, 32, 33, 35),
+    (13, 22, 35, 27, 34, 36, 37, 38),
+    (24, 29, 35, 28, 34, 37, 38, 39),
 )
-SEND_ON = (3, 6, 9, 10, 14, 15)
+SEND_ON = (3, 5, 6, 7, 8, 11)
 
 
 def code(v):
@@ -77,9 +78,13 @@
 
     mid = DEPTH // 2
     lo, hi, every = pl.ds(0, mid), pl.ds(mid, mid), pl.ds(0, DEPTH)
+    most, rest = pl.ds(0, 3 * DEPTH // 4), pl.ds(3 * DEPTH // 4, DEPTH // 4)
     left, right = pl.ds(0, 128), pl.ds(128, 128)
     s_moves = [
-        remote(sall.at[i, r0, c0], sall.at[j, r0, c1], s_ss.at[n], s_rs.at[n], device)
+        remote(
+            s_hbm.at[r0, c0] if i == 0 else sall.at[i, r0, c0],
+            sall.at[j, r0, c1], s_ss.at[n], s_rs.at[n], device,
+        )
         for n, (i, j, r0, c0, c1, device) in enumerate((
             (0, 1, every, left, left, y_up),
             (0, 1, every, left, right, y_dn),
@@ -93,14 +98,16 @@
             (2, 4, hi, right, right, y_dn),
             (3, 5, every, left, left, y_up),
             (3, 5, every, left, right, y_dn),
-            (3, 6, every, right, left, y_up),
-            (3, 6, every, right, right, y_dn),
+            (3, 6, most, right, left, y_up),
+            (3, 6, most, right, right, y_dn),
             (4, 7, every, left, left, x_far),
             (4, 7, every, right, right, x_far),
+            (2, 6, rest, left, left, x_far),
+            (2, 6, rest, right, right, x_far),
         ))
     ]
     passes = [
-        ((0, 1), (6, 7)), ((2, 3), (8, 9)), ((4,), (10, 11)), ((5,), (12, 13)), ((6, 7), (14,)),
+        ((0, 1), (6, 7)), ((2, 3), (8, 9, 16, 17)), ((4,), (10, 11)), ((5,), (12, 13)), ((6, 7), (14,)),
         ((8, 9), (15,)),
     ]
     dy = (z // 2 + 4 - y) % 4
@@ -114,10 +121,10 @@
         in_sem.at[2],
     )
     c_in.start()
-    s_in.wait()
     pl.semaphore_wait(barrier, 9)
     for i in (0, 1, 4, 2, 3, 5):
         s_moves[i].start()
+    s_in.wait()
 
     c_in.wait()
     cmd_t[...] = cpad[...].T
@@ -207,6 +214,9 @@
             def _(slot=slot):
                 s_moves[2 * slot].wait_recv()
                 s_moves[2 * slot + 1].wait_recv()
+                if slot == 6:
+                    s_moves[16].wait_recv()
+                    s_moves[17].wait_recv()
 
         mine = (g == my_slot).astype(jnp.float32)
         tile = 512
@@ -276,12 +286,15 @@
             out_4(g, d).start()
             out_3(g, d).start()
 
-    def add_gradient(g, start):
+    scale_factor = 1.0 / jnp.sqrt(jnp.float32(2048))
+
+    def add_gradient(g, start, when):
         here = rows(start, HALF)
-        g_ref[here, :] += lax.dot_general(
+        added = g_ref[here, :] + lax.dot_general(
             rall[g, here, :], sall[g], (((1,), (1,)), ((), ())),
             preferred_element_type=jnp.float32,
         )
+        g_ref[here, :] = added * jnp.where(g == when.index(max(when)), scale_factor, 1.0)
 
     def stage_6(g):
         for d in (0, 1):
@@ -289,11 +302,11 @@
             in_3(g, d).wait_recv()
             in_4(g, d).wait_recv()
         out_core(g).start()
-        add_gradient(g, own0)
+        add_gradient(g, own0, WHEN[6])
 
     def stage_gradient(g):
         in_core(g).wait_recv()
-        add_gradient(g, other0)
+        add_gradient(g, other0, WHEN[7])
 
         @pl.when(g == my_slot)
         def _():
@@ -331,6 +344,18 @@
     lax.fori_loop(0, max(WHEN[-1]) + 1, tick, 0)
     for move in s_moves:
         move.wait_send()
+
+
+def finish(g_ref, res_ref, g_hbm, res_hbm, sem):
+    size = FULL // PIECES
+    moves = [pltpu.make_async_copy(res_ref, res_hbm, sem.at[PIECES])]
+    for i in range(PIECES):
+        here = pl.ds(i * size, size)
+        moves.append(pltpu.make_async_copy(g_ref.at[here], g_hbm.at[here], sem.at[i]))
+    for move in moves:
+        move.start()
+    for move in moves:
+        move.wait()
 
 
 def on_device(reconstructor, slopes, commands):
@@ -362,8 +387,8 @@
             vmem((BLOCKS, FULL, BLOCK), jnp.bfloat16),
             vmem((128, FULL), jnp.float32),
             pltpu.SemaphoreType.DMA((3,)),
-            pltpu.SemaphoreType.DMA((16,)),
-            pltpu.SemaphoreType.DMA((16,)),
+            pltpu.SemaphoreType.DMA((18,)),
+            pltpu.SemaphoreType.DMA((18,)),
             pltpu.SemaphoreType.DMA((BLOCKS, 17)),
             pltpu.SemaphoreType.DMA((BLOCKS, 17)),
         ],
@@ -374,8 +399,19 @@
             flops=4 * 2048 * FULL * DEPTH, bytes_accessed=9 << 20, transcendentals=0
         ),
     )(reconstructor, slopes, commands)
-    scale_factor = 1.0 / jnp.sqrt(jnp.float32(2048))
-    return gradient * scale_factor, residual
+    return pl.pallas_call(
+        finish,
+        out_shape=(
+            jax.ShapeDtypeStruct((FULL, DEPTH), jnp.float32),
+            jax.ShapeDtypeStruct((64, FULL), jnp.float32),
+        ),
+        in_specs=[pl.BlockSpec(memory_space=pltpu.VMEM)] * 2,
+        out_specs=[pl.BlockSpec(memory_space=pl.ANY)] * 2,
+        scratch_shapes=[
+            pltpu.SemaphoreType.DMA((PIECES + 1,)),
+        ],
+        compiler_params=pltpu.CompilerParams(vmem_limit_bytes=4 << 20),
+    )(gradient, residual)
 
 
 def solution(mesh):

time: 91.1 us -> 89.3 us (0.980)
  other arithmetic: 2.86 us -> 0 us
  Pallas kernels: 86.8 us -> 88.6 us
    mul x1 -> x0, other arithmetic: 2.86 us -> none  [on_device(): return (gradient * scale_factor, residual)]
    pallas_call x0 -> x1, Pallas kernels: none -> 2.49 us  [on_device(): pl.pallas_call(finish, out_shape=(jax.ShapeDtypeStruct((FULL, DEPTH), jnp...]
where the time goes in v3:
time: 89.3 us; the launch traced here: 89.2 us
  Pallas kernels  88.6 us (99%)
    pallas_call x1, Pallas kernels, on_device(): pl.pallas_call(kernel, out_shape=(pltpu.VMEM((FULL, DEPTH), jnp.float32),...  86.1 us
    pallas_call x1, Pallas kernels, on_device(): pl.pallas_call(finish, out_shape=(jax.ShapeDtypeStruct((FULL, DEPTH), jnp...  2.49 us

profile of v3, /device:TPU:1, one launch (start us, length us, event | category | flops | bytes accessed | tf_op | source)
XLA Modules:
  0.0 89.2 jit_solution(14044471658403050572)
XLA Ops:
  0.6 86.1 %shard_map.50 = (f32[1024,1280]{1,0:T(8,128)S(1)}, f32[64,1024]{1,0:T(8,128)S(1)}) custom-call(bf16[1024,1280]{1,0:T(8,128)(2,1)} %r_hbm.1, bf16[1280,256]{1,0:T(8,128)(2,1)} %s_hbm.1, f32[64,1024]{1,0:T(8,128)} %c_hbm.1), custom_call_target="tpu_custom_call" | custom-call | flops 10737418240 | bytes 9437184 | tf_op jit(solution)/shard_map/pallas_call | solution.py:363
  86.7 2.5 %shard_map.51 = (f32[1024,1280]{1,0:T(8,128)}, f32[64,1024]{1,0:T(8,128)}) custom-call(f32[1024,1280]{1,0:T(8,128)S(1)} %get-tuple-element.4.g_ref, f32[64,1024]{1,0:T(8,128)S(1)} %get-tuple-element.5.res_ref), custom_call_target="tpu_custom_call" | custom-call | tf_op jit(solution)/shard_map/pallas_call | solution.py:402

commit v4 on v3

--- a/solution.py
+++ b/solution.py
@@ -16,17 +16,29 @@
 BLOCK = 256
 BLOCKS = 8
 PIECES = 8
-WHEN = (
-    (0, 3, 5, 8, 11, 14, 16, 19),
-    (1, 4, 8, 9, 12, 15, 17, 20),
-    (2, 7, 12, 13, 15, 19, 21, 23),
-    (4, 10, 22, 16, 18, 24, 25, 30),
-    (5, 14, 23, 19, 22, 28, 27, 31),
-    (9, 17, 30, 23, 26, 32, 33, 35),
-    (13, 22, 35, 27, 34, 36, 37, 38),
-    (24, 29, 35, 28, 34, 37, 38, 39),
+KINDS = {
+    "two": (0, 7,),
+    "xf": (1, 6,),
+    "ring": (2, 3, 4, 5,),
+}
+ORDER = (
+    ("predict", 0), ("two_1", 0), ("two_2", 0), ("pass_on", 0), ("predict", 1), ("xf_1", 1),
+    ("two_3", 0), ("pass_on", 1), ("predict", 2), ("pass_on", 2), ("pass_on", 3), ("predict", 3),
+    ("ring_1", 2), ("pass_on", 4), ("ring_1", 3), ("xf_2", 1), ("ring_2", 2), ("two_4", 0),
+    ("pass_on", 5), ("predict", 4), ("ring_1", 4), ("ring_3", 2), ("ring_2", 3), ("xf_3", 1),
+    ("two_5", 0), ("ring_2", 4), ("ring_4", 2), ("ring_3", 3), ("predict", 5), ("ring_1", 5),
+    ("ring_5", 2), ("ring_3", 4), ("xf_4", 1), ("ring_4", 3), ("predict", 6), ("ring_2", 5),
+    ("ring_4", 4), ("xf_1", 6), ("ring_6", 2), ("xf_5", 1), ("predict", 7), ("ring_3", 5),
+    ("two_1", 7), ("ring_5", 4), ("ring_7", 2), ("ring_5", 3), ("ring_4", 5), ("xf_2", 6),
+    ("xf_6", 1), ("ring_6", 4), ("ring_6", 3), ("two_2", 7), ("ring_8", 2), ("two_6", 0),
+    ("ring_5", 5), ("xf_3", 6), ("ring_7", 4), ("ring_7", 3), ("xf_7", 1), ("ring_6", 5),
+    ("ring_9", 2), ("gradient", 1), ("xf_4", 6), ("ring_8", 4), ("two_3", 7), ("ring_8", 3),
+    ("ring_7", 5), ("ring_10", 2), ("xf_5", 6), ("two_4", 7), ("ring_9", 4), ("ring_9", 3),
+    ("gradient", 0), ("ring_8", 5), ("gradient", 2), ("xf_6", 6), ("two_5", 7), ("ring_10", 4),
+    ("ring_10", 3), ("ring_9", 5), ("gradient", 4), ("gradient", 3), ("xf_7", 6), ("two_6", 7),
+    ("ring_10", 5), ("gradient", 6), ("gradient", 7), ("gradient", 5),
 )
-SEND_ON = (3, 5, 6, 7, 8, 11)
+LAST_OWN, LAST_OTHER = 5, 5
 
 
 def code(v):
@@ -44,7 +56,7 @@
 def kernel(
     r_hbm, s_hbm, c_hbm, g_ref, res_ref,
     r_ref, sall, cpad, cmd_t, acc, csend, crecv, near_s, near_r, far_s, far_r, sum_s, sum_r,
-    xsend, xrecv, rall, turned,
+    ring_s, ring_r, xsend, xrecv, rall, turned,
     in_sem, s_ss, s_rs, ss, rs,
 ):
     row, col = lax.axis_index("row"), lax.axis_index("col")
@@ -137,56 +149,10 @@
     def rows(start, size):
         return pl.ds(pl.multiple_of(start, size), size)
 
-    def part(at, size=SLICE, skip=0):
-        return rows(((z + at + 8) % 8) * SLICE + skip, size)
-
-    def full_part(at, size=SLICE, skip=0):
-        return rows(own0 + ((z + at + 8) % 8) * SLICE + skip, size)
-
     def core_move(g):
         return remote(csend.at[g], crecv.at[g], ss.at[g, 0], rs.at[g, 0], twin)
 
     one, two = (z_up, z_dn), (z_up2, z_dn2)
-
-    def near_move(g, d):
-        return remote(near_s.at[g, d], near_r.at[g, d], ss.at[g, 1 + d], rs.at[g, 1 + d], one[d])
-
-    def far_move(g, d):
-        return remote(far_s.at[g, d], far_r.at[g, d], ss.at[g, 3 + d], rs.at[g, 3 + d], two[d])
-
-    def sum_move(g, d):
-        return remote(sum_s.at[g, d], sum_r.at[g, d], ss.at[g, 5 + d], rs.at[g, 5 + d], two[d])
-
-    def x_move(g):
-        return remote(xsend.at[g], xrecv.at[g], ss.at[g, 7], rs.at[g, 7], x_near)
-
-    def spread(g, d, n, at, device, size=SLICE, skip=0):
-        here = rall.at[g, full_part(at, size, skip)]
-        return remote(here, here, ss.at[g, n + d], rs.at[g, n + d], device)
-
-    def out_1(g, d):
-        return spread(g, d, 8, 0, one[d])
-
-    def in_1(g, d):
-        return spread(g, d, 8, (-1, 1)[d], one[d])
-
-    def out_2(g, d):
-        return spread(g, d, 10, 0, two[d])
-
-    def in_2(g, d):
-        return spread(g, d, 10, (-2, 2)[d], two[d])
-
-    def out_3(g, d):
-        return spread(g, d, 12, (-2, 2)[d], one[d])
-
-    def in_3(g, d):
-        return spread(g, d, 12, (-3, 3)[d], one[d])
-
-    def out_4(g, d):
-        return spread(g, d, 14, (-2, 2)[d], two[d], SLICE // 2, d * SLICE // 2)
-
-    def in_4(g, d):
-        return spread(g, d, 14, 4, two[d], SLICE // 2, d * SLICE // 2)
 
     def out_core(g):
         here = rall.at[g, rows(own0, HALF)]
@@ -195,10 +161,6 @@
     def in_core(g):
         here = rall.at[g, rows(other0, HALF)]
         return remote(here, here, ss.at[g, 16], rs.at[g, 16], twin)
-
-    def both(g, at, size=SLICE, skip=0):
-        here = part(at, size, skip)
-        return acc[g, here, :] + decode(crecv[g, here, :])
 
     def pass_on(n):
         arrived, onward = passes[n]
@@ -208,15 +170,12 @@
             s_moves[i].start()
 
     def stage_predict(g):
-        for slot in (5, 6, 7):
-
-            @pl.when(g == slot)
-            def _(slot=slot):
-                s_moves[2 * slot].wait_recv()
-                s_moves[2 * slot + 1].wait_recv()
-                if slot == 6:
-                    s_moves[16].wait_recv()
-                    s_moves[17].wait_recv()
+        if g >= 5:
+            s_moves[2 * g].wait_recv()
+            s_moves[2 * g + 1].wait_recv()
+        if g == 6:
+            s_moves[16].wait_recv()
+            s_moves[17].wait_recv()
 
         mine = (g == my_slot).astype(jnp.float32)
         tile = 512
@@ -237,76 +196,296 @@
         def _(i):
             acc[g, rows(i * tile, tile), :] = predicted(own0 + i * tile)
 
-    half = SLICE // 2
-    first, second = pl.ds(0, SLICE), pl.ds(SLICE, SLICE)
-
-    def stage_1(g):
-        core_move(g).wait_recv()
-        for d, sign in ((0, 1), (1, -1)):
-            far_s[g, d] = code(both(g, 4, half, d * half))
-            far_move(g, d).start()
-            near_s[g, d, second, :] = code(both(g, 3 * sign))
-            near_s[g, d, first, :] = code(both(g, sign))
-            near_move(g, d).start()
-
-    def stage_2(g):
-        for d, sign in ((0, 1), (1, -1)):
-            near_move(g, d).wait_recv()
-            far_move(g, d).wait_recv()
-            for h in (0, 1):
-                total = both(g, 2 * sign, half, h * half) + decode(
-                    near_r[g, d, pl.ds(SLICE + h * half, half), :]
-                )
-                if h == d:
-                    total = total + decode(far_r[g, d])
-                sum_s[g, d, pl.ds(h * half, half), :] = code(total)
-            sum_move(g, d).start()
-
-    def stage_3(g):
-        total = both(g, 0) + decode(near_r[g, 0, first, :]) + decode(near_r[g, 1, first, :])
-        for d in (0, 1):
-            sum_move(g, d).wait_recv()
-            total = total + decode(sum_r[g, d])
-        acc[g, part(0), :] = total
-        xsend[g] = code(total)
-        x_move(g).start()
-
-    def stage_4(g):
-        x_move(g).wait_recv()
-        low = (acc[g, part(0), :] + decode(xrecv[g])).astype(jnp.bfloat16)
-        rall[g, full_part(0), :] = low
-        for d in (0, 1):
-            out_2(g, d).start()
-        for d in (0, 1):
-            out_1(g, d).start()
-
-    def stage_5(g):
-        for d in (0, 1):
-            in_2(g, d).wait_recv()
-            out_4(g, d).start()
-            out_3(g, d).start()
-
     scale_factor = 1.0 / jnp.sqrt(jnp.float32(2048))
 
-    def add_gradient(g, start, when):
+    def add_gradient(g, start, last):
         here = rows(start, HALF)
         added = g_ref[here, :] + lax.dot_general(
             rall[g, here, :], sall[g], (((1,), (1,)), ((), ())),
             preferred_element_type=jnp.float32,
         )
-        g_ref[here, :] = added * jnp.where(g == when.index(max(when)), scale_factor, 1.0)
-
-    def stage_6(g):
-        for d in (0, 1):
-            in_1(g, d).wait_recv()
-            in_3(g, d).wait_recv()
-            in_4(g, d).wait_recv()
+        g_ref[here, :] = added * scale_factor if g == last else added
+
+    def share(g):
         out_core(g).start()
-        add_gradient(g, own0, WHEN[6])
+        add_gradient(g, own0, LAST_OWN)
+
+    def with_twin(g, here):
+        return acc[g, here, :] + decode(crecv[g, here, :])
+
+    def tree(size, base, term):
+        half = size // 2
+        first, second = pl.ds(0, size), pl.ds(size, size)
+
+        def part(at, count=size, skip=0):
+            return rows(base + ((z + at + 8) % 8) * size + skip, count)
+
+        def near_move(g, d):
+            here = near_s.at[g, d, pl.ds(0, 2 * size)]
+            there = near_r.at[g, d, pl.ds(0, 2 * size)]
+            return remote(here, there, ss.at[g, 1 + d], rs.at[g, 1 + d], one[d])
+
+        def far_move(g, d):
+            here, there = far_s.at[g, d, pl.ds(0, half)], far_r.at[g, d, pl.ds(0, half)]
+            return remote(here, there, ss.at[g, 3 + d], rs.at[g, 3 + d], two[d])
+
+        def sum_move(g, d):
+            here, there = sum_s.at[g, d, first], sum_r.at[g, d, first]
+            return remote(here, there, ss.at[g, 5 + d], rs.at[g, 5 + d], two[d])
+
+        def spread(g, d, n, at, device, count=size, skip=0):
+            start = own0 + base + ((z + at + 8) % 8) * size + skip
+            here = rall.at[g, rows(start, count)]
+            return remote(here, here, ss.at[g, n + d], rs.at[g, n + d], device)
+
+        def out_1(g, d):
+            return spread(g, d, 8, 0, one[d])
+
+        def in_1(g, d):
+            return spread(g, d, 8, (-1, 1)[d], one[d])
+
+        def out_2(g, d):
+            return spread(g, d, 10, 0, two[d])
+
+        def in_2(g, d):
+            return spread(g, d, 10, (-2, 2)[d], two[d])
+
+        def out_3(g, d):
+            return spread(g, d, 12, (-2, 2)[d], one[d])
+
+        def in_3(g, d):
+            return spread(g, d, 12, (-3, 3)[d], one[d])
+
+        def out_4(g, d):
+            return spread(g, d, 14, (-2, 2)[d], two[d], half, d * half)
+
+        def in_4(g, d):
+            return spread(g, d, 14, 4, two[d], half, d * half)
+
+        def send_terms(g):
+            for d, sign in ((0, 1), (1, -1)):
+                far_s[g, d, pl.ds(0, half), :] = code(term(g, part(4, half, d * half)))
+                far_move(g, d).start()
+                near_s[g, d, second, :] = code(term(g, part(3 * sign)))
+                near_s[g, d, first, :] = code(term(g, part(sign)))
+                near_move(g, d).start()
+
+        def send_sums(g):
+            for d, sign in ((0, 1), (1, -1)):
+                near_move(g, d).wait_recv()
+                far_move(g, d).wait_recv()
+                for h in (0, 1):
+                    total = term(g, part(2 * sign, half, h * half)) + decode(
+                        near_r[g, d, pl.ds(size + h * half, half), :]
+                    )
+                    if h == d:
+                        total = total + decode(far_r[g, d, pl.ds(0, half), :])
+                    sum_s[g, d, pl.ds(h * half, half), :] = code(total)
+                sum_move(g, d).start()
+
+        def total(g):
+            total = term(g, part(0))
+            for d in (0, 1):
+                sum_move(g, d).wait_recv()
+                total = total + decode(near_r[g, d, first, :]) + decode(sum_r[g, d, first, :])
+            return total
+
+        def hand_round(g, residual):
+            rall[g, rows(own0 + base + z * size, size), :] = residual.astype(jnp.bfloat16)
+            for d in (0, 1):
+                out_2(g, d).start()
+            for d in (0, 1):
+                out_1(g, d).start()
+
+        def hand_on(g):
+            for d in (0, 1):
+                in_2(g, d).wait_recv()
+                out_4(g, d).start()
+                out_3(g, d).start()
+
+        def all_here(g):
+            for d in (0, 1):
+                in_1(g, d).wait_recv()
+                in_3(g, d).wait_recv()
+                in_4(g, d).wait_recv()
+
+        def sent(g):
+            for move in (near_move, far_move, sum_move, out_1, out_2, out_3, out_4):
+                for d in (0, 1):
+                    move(g, d).wait_send()
+
+        return part, send_terms, send_sums, total, hand_round, hand_on, all_here, sent
+
+    def x_move(g):
+        here, there = xsend.at[g, pl.ds(0, SLICE)], xrecv.at[g, pl.ds(0, SLICE)]
+        return remote(here, there, ss.at[g, 18], rs.at[g, 18], x_near)
+
+    (
+        two_part, two_terms, two_sums, two_total, two_round, two_on, two_here, two_sent,
+    ) = tree(SLICE, 0, with_twin)
+
+    def two_1(g):
+        core_move(g).wait_recv()
+        two_terms(g)
+
+    def two_3(g):
+        total = two_total(g)
+        acc[g, two_part(0), :] = total
+        xsend[g, pl.ds(0, SLICE), :] = code(total)
+        x_move(g).start()
+
+    def two_4(g):
+        x_move(g).wait_recv()
+        two_round(g, acc[g, two_part(0), :] + decode(xrecv[g, pl.ds(0, SLICE), :]))
+
+    def two_6(g):
+        two_here(g)
+        share(g)
+
+    quarter = HALF // 2
+
+    def half_move(g):
+        return remote(xsend.at[g], xrecv.at[g], ss.at[g, 7], rs.at[g, 7], x_near)
+
+    def out_x(g):
+        here = rall.at[g, rows(own0 + xl * quarter, quarter)]
+        return remote(here, here, ss.at[g, 17], rs.at[g, 17], x_near)
+
+    def in_x(g):
+        here = rall.at[g, rows(own0 + (1 - xl) * quarter, quarter)]
+        return remote(here, here, ss.at[g, 17], rs.at[g, 17], x_near)
+
+    xf_part, xf_terms, xf_sums, xf_total, xf_round, xf_on, xf_here, xf_sent = tree(
+        SLICE // 2, xl * quarter, lambda g, here: acc[g, here, :]
+    )
+
+    def xf_1(g):
+        core_move(g).wait_recv()
+
+        @pl.loop(0, quarter // SLICE)
+        def _(i):
+            here = rows((1 - xl) * quarter + i * SLICE, SLICE)
+            xsend[g, rows(i * SLICE, SLICE), :] = code(with_twin(g, here))
+
+        half_move(g).start()
+
+    def xf_2(g):
+        half_move(g).wait_recv()
+
+        @pl.loop(0, quarter // SLICE)
+        def _(i):
+            here = rows(xl * quarter + i * SLICE, SLICE)
+            other = decode(xrecv[g, rows(i * SLICE, SLICE), :])
+            acc[g, here, :] = with_twin(g, here) + other
+
+        xf_terms(g)
+
+    def xf_4(g):
+        xf_round(g, xf_total(g))
+
+    def xf_6(g):
+        xf_here(g)
+        out_x(g).start()
+
+    def xf_7(g):
+        in_x(g).wait_recv()
+        share(g)
+
+    def ring_part(at):
+        return rows(((z + at + 8) % 8) * SLICE, SLICE)
+
+    def ring_here(g, at):
+        return rall.at[g, rows(own0 + ((z + at + 8) % 8) * SLICE, SLICE)]
+
+    def up_move(g, i):
+        return remote(ring_s.at[g, i], ring_r.at[g, i], ss.at[g, 1 + i], rs.at[g, 1 + i], z_up)
+
+    def dn_move(g, i):
+        return remote(
+            ring_s.at[g, 4 + i], ring_r.at[g, 4 + i], ss.at[g, 5 + i], rs.at[g, 5 + i], z_dn
+        )
+
+    def out_up(g, i):
+        here = ring_here(g, -i)
+        return remote(here, here, ss.at[g, 9 + i], rs.at[g, 9 + i], z_up)
+
+    def in_up(g, i):
+        here = ring_here(g, -i - 1)
+        return remote(here, here, ss.at[g, 9 + i], rs.at[g, 9 + i], z_up)
+
+    def out_dn(g, i):
+        here = ring_here(g, i)
+        return remote(here, here, ss.at[g, 12 + i], rs.at[g, 12 + i], z_dn)
+
+    def in_dn(g, i):
+        here = ring_here(g, i + 1)
+        return remote(here, here, ss.at[g, 12 + i], rs.at[g, 12 + i], z_dn)
+
+    def send_up(g, i):
+        total = with_twin(g, ring_part(4 - i))
+        if i:
+            up_move(g, i - 1).wait_recv()
+            total = total + decode(ring_r[g, i - 1])
+        ring_s[g, i] = code(total)
+        up_move(g, i).start()
+
+    def send_dn(g, i):
+        total = with_twin(g, ring_part(i - 3))
+        if i:
+            dn_move(g, i - 1).wait_recv()
+            total = total + decode(ring_r[g, 3 + i])
+        ring_s[g, 4 + i] = code(total)
+        dn_move(g, i).start()
+
+    def ring_1(g):
+        core_move(g).wait_recv()
+        send_up(g, 0)
+
+    def ring_2(g, i=1):
+        send_dn(g, i - 1)
+        send_up(g, i)
+
+    def ring_5(g):
+        dn_move(g, 2).wait_recv()
+        up_move(g, 3).wait_recv()
+        total = with_twin(g, ring_part(0)) + decode(ring_r[g, 6]) + decode(ring_r[g, 3])
+        acc[g, ring_part(0), :] = total
+        xsend[g, pl.ds(0, SLICE), :] = code(total)
+        x_move(g).start()
+
+    def ring_6(g):
+        x_move(g).wait_recv()
+        low = acc[g, ring_part(0), :] + decode(xrecv[g, pl.ds(0, SLICE), :])
+        rall[g, rows(own0 + z * SLICE, SLICE), :] = low.astype(jnp.bfloat16)
+        out_dn(g, 0).start()
+        out_up(g, 0).start()
+
+    def ring_7(g, i=0):
+        in_dn(g, i).wait_recv()
+        out_dn(g, i + 1).start()
+        in_up(g, i).wait_recv()
+        out_up(g, i + 1).start()
+
+    def ring_9(g):
+        in_dn(g, 2).wait_recv()
+        out_dn(g, 3).start()
+        in_up(g, 2).wait_recv()
+
+    def ring_10(g):
+        in_dn(g, 3).wait_recv()
+        share(g)
+
+    def ring_sent(g):
+        for i in range(4):
+            up_move(g, i).wait_send()
+            out_dn(g, i).wait_send()
+        for i in range(3):
+            dn_move(g, i).wait_send()
+            out_up(g, i).wait_send()
 
     def stage_gradient(g):
         in_core(g).wait_recv()
-        add_gradient(g, other0, WHEN[7])
+        add_gradient(g, other0, LAST_OTHER)
 
         @pl.when(g == my_slot)
         def _():
@@ -315,33 +494,36 @@
             res_ref[...] = turned[rows(core * 64, 64), :]
 
         core_move(g).wait_send()
-        for move in (near_move, far_move, sum_move, out_1, out_2, out_3, out_4):
-            for d in (0, 1):
-                move(g, d).wait_send()
-        x_move(g).wait_send()
         out_core(g).wait_send()
 
-    stages = [
-        stage_predict, stage_1, stage_2, stage_3, stage_4, stage_5, stage_6, stage_gradient,
-    ]
-    order = [6, 5, 4, 3, 2, 1, 0, 7]
-
-    def tick(t, carry):
-        for n, at in enumerate(SEND_ON):
-            pl.when(t == at)(functools.partial(pass_on, n))
-        for k in order:
-            g, active = jnp.int32(0), t == WHEN[k][0]
-            for i in range(1, BLOCKS):
-                g = jnp.where(t == WHEN[k][i], i, g)
-                active = active | (t == WHEN[k][i])
-
-            @pl.when(active)
-            def _(k=k, g=g):
-                stages[k](g)
-
-        return carry
-
-    lax.fori_loop(0, max(WHEN[-1]) + 1, tick, 0)
+        if g in KINDS["two"]:
+            two_sent(g)
+            x_move(g).wait_send()
+
+        if g in KINDS["xf"]:
+            xf_sent(g)
+            half_move(g).wait_send()
+            out_x(g).wait_send()
+
+        if g in KINDS["ring"]:
+            ring_sent(g)
+            x_move(g).wait_send()
+
+    stages = {
+        "pass_on": pass_on, "predict": stage_predict, "gradient": stage_gradient,
+        "two_1": two_1, "two_2": two_sums, "two_3": two_3, "two_4": two_4, "two_5": two_on,
+        "two_6": two_6,
+        "xf_1": xf_1, "xf_2": xf_2, "xf_3": xf_sums, "xf_4": xf_4, "xf_5": xf_on, "xf_6": xf_6,
+        "xf_7": xf_7,
+        "ring_1": ring_1, "ring_2": ring_2, "ring_3": functools.partial(ring_2, i=2),
+        "ring_4": functools.partial(ring_2, i=3), "ring_5": ring_5, "ring_6": ring_6,
+        "ring_7": ring_7, "ring_8": functools.partial(ring_7, i=1), "ring_9": ring_9,
+        "ring_10": ring_10,
+    }
+
+    for name, g in ORDER:
+        stages[name](g)
+
     for move in s_moves:
         move.wait_send()
 
@@ -382,15 +564,17 @@
             vmem((BLOCKS, 2, SLICE // 2, BLOCK), jnp.bfloat16),
             vmem((BLOCKS, 2, SLICE, BLOCK), jnp.bfloat16),
             vmem((BLOCKS, 2, SLICE, BLOCK), jnp.bfloat16),
-            vmem((BLOCKS, SLICE, BLOCK), jnp.bfloat16),
-            vmem((BLOCKS, SLICE, BLOCK), jnp.bfloat16),
+            vmem((BLOCKS, 7, SLICE, BLOCK), jnp.bfloat16),
+            vmem((BLOCKS, 7, SLICE, BLOCK), jnp.bfloat16),
+            vmem((BLOCKS, HALF // 2, BLOCK), jnp.bfloat16),
+            vmem((BLOCKS, HALF // 2, BLOCK), jnp.bfloat16),
             vmem((BLOCKS, FULL, BLOCK), jnp.bfloat16),
             vmem((128, FULL), jnp.float32),
             pltpu.SemaphoreType.DMA((3,)),
             pltpu.SemaphoreType.DMA((18,)),
             pltpu.SemaphoreType.DMA((18,)),
-            pltpu.SemaphoreType.DMA((BLOCKS, 17)),
-            pltpu.SemaphoreType.DMA((BLOCKS, 17)),
+            pltpu.SemaphoreType.DMA((BLOCKS, 19)),
+            pltpu.SemaphoreType.DMA((BLOCKS, 19)),
         ],
         compiler_params=pltpu.CompilerParams(
             collective_id=0, has_side_effects=True, vmem_limit_bytes=56 << 20

time: 89.3 us -> 86.9 us (0.973)
  Pallas kernels: 88.6 us -> 86 us
    pallas_call x1, Pallas kernels: 86.1 us -> 83.5 us  [on_device(): pl.pallas_call(kernel, out_shape=(pltpu.VMEM((FULL, DEPTH), jnp.float32),...]
where the time goes in v4:
time: 86.9 us; the launch traced here: 86.8 us
  Pallas kernels  86 us (99%)
    pallas_call x1, Pallas kernels, on_device(): pl.pallas_call(kernel, out_shape=(pltpu.VMEM((FULL, DEPTH), jnp.float32),...  83.5 us
    pallas_call x1, Pallas kernels, on_device(): pl.pallas_call(finish, out_shape=(jax.ShapeDtypeStruct((FULL, DEPTH), jnp...  2.49 us

profile of v4, /device:TPU:1, one launch (start us, length us, event | category | flops | bytes accessed | tf_op | source)
XLA Modules:
  0.0 86.8 jit_solution(7448944686163557947)
XLA Ops:
  0.6 83.5 %shard_map.50 = (f32[1024,1280]{1,0:T(8,128)S(1)}, f32[64,1024]{1,0:T(8,128)S(1)}) custom-call(bf16[1024,1280]{1,0:T(8,128)(2,1)} %r_hbm.1, bf16[1280,256]{1,0:T(8,128)(2,1)} %s_hbm.1, f32[64,1024]{1,0:T(8,128)} %c_hbm.1), custom_call_target="tpu_custom_call" | custom-call | flops 10737418240 | bytes 9437184 | tf_op jit(solution)/shard_map/pallas_call | solution.py:545
  84.2 2.5 %shard_map.51 = (f32[1024,1280]{1,0:T(8,128)}, f32[64,1024]{1,0:T(8,128)}) custom-call(f32[1024,1280]{1,0:T(8,128)S(1)} %get-tuple-element.4.g_ref, f32[64,1024]{1,0:T(8,128)S(1)} %get-tuple-element.5.res_ref), custom_call_target="tpu_custom_call" | custom-call | tf_op jit(solution)/shard_map/pallas_call | solution.py:586

commit v5 on v4

--- a/solution.py
+++ b/solution.py
@@ -22,20 +22,20 @@
     "ring": (2, 3, 4, 5,),
 }
 ORDER = (
-    ("predict", 0), ("two_1", 0), ("two_2", 0), ("pass_on", 0), ("predict", 1), ("xf_1", 1),
-    ("two_3", 0), ("pass_on", 1), ("predict", 2), ("pass_on", 2), ("pass_on", 3), ("predict", 3),
-    ("ring_1", 2), ("pass_on", 4), ("ring_1", 3), ("xf_2", 1), ("ring_2", 2), ("two_4", 0),
-    ("pass_on", 5), ("predict", 4), ("ring_1", 4), ("ring_3", 2), ("ring_2", 3), ("xf_3", 1),
-    ("two_5", 0), ("ring_2", 4), ("ring_4", 2), ("ring_3", 3), ("predict", 5), ("ring_1", 5),
-    ("ring_5", 2), ("ring_3", 4), ("xf_4", 1), ("ring_4", 3), ("predict", 6), ("ring_2", 5),
-    ("ring_4", 4), ("xf_1", 6), ("ring_6", 2), ("xf_5", 1), ("predict", 7), ("ring_3", 5),
-    ("two_1", 7), ("ring_5", 4), ("ring_7", 2), ("ring_5", 3), ("ring_4", 5), ("xf_2", 6),
-    ("xf_6", 1), ("ring_6", 4), ("ring_6", 3), ("two_2", 7), ("ring_8", 2), ("two_6", 0),
-    ("ring_5", 5), ("xf_3", 6), ("ring_7", 4), ("ring_7", 3), ("xf_7", 1), ("ring_6", 5),
-    ("ring_9", 2), ("gradient", 1), ("xf_4", 6), ("ring_8", 4), ("two_3", 7), ("ring_8", 3),
-    ("ring_7", 5), ("ring_10", 2), ("xf_5", 6), ("two_4", 7), ("ring_9", 4), ("ring_9", 3),
-    ("gradient", 0), ("ring_8", 5), ("gradient", 2), ("xf_6", 6), ("two_5", 7), ("ring_10", 4),
-    ("ring_10", 3), ("ring_9", 5), ("gradient", 4), ("gradient", 3), ("xf_7", 6), ("two_6", 7),
+    ("predict", 0), ("two_1", 0), ("pass_on", 0), ("two_2", 0), ("predict", 1), ("xf_1", 1),
+    ("pass_on", 1), ("pass_on", 2), ("pass_on", 3), ("predict", 2), ("two_3", 0), ("ring_1", 2),
+    ("xf_2", 1), ("predict", 3), ("pass_on", 4), ("ring_2", 2), ("ring_1", 3), ("pass_on", 5),
+    ("predict", 4), ("xf_3", 1), ("ring_1", 4), ("ring_3", 2), ("two_4", 0), ("ring_2", 3),
+    ("ring_2", 4), ("ring_4", 2), ("xf_4", 1), ("predict", 5), ("ring_1", 5), ("ring_3", 3),
+    ("ring_3", 4), ("two_5", 0), ("ring_5", 2), ("xf_5", 1), ("predict", 6), ("ring_2", 5),
+    ("ring_4", 3), ("xf_1", 6), ("ring_4", 4), ("ring_6", 2), ("predict", 7), ("ring_3", 5),
+    ("ring_5", 3), ("two_1", 7), ("ring_5", 4), ("xf_2", 6), ("ring_4", 5), ("xf_6", 1),
+    ("ring_6", 4), ("ring_7", 2), ("ring_6", 3), ("xf_3", 6), ("ring_5", 5), ("two_2", 7),
+    ("ring_7", 4), ("two_6", 0), ("ring_8", 2), ("xf_7", 1), ("ring_7", 3), ("xf_4", 6),
+    ("ring_6", 5), ("gradient", 0), ("ring_8", 4), ("two_3", 7), ("ring_9", 2), ("ring_8", 3),
+    ("xf_5", 6), ("gradient", 1), ("ring_7", 5), ("ring_9", 4), ("two_4", 7), ("ring_10", 2),
+    ("xf_6", 6), ("ring_8", 5), ("gradient", 2), ("ring_9", 3), ("two_5", 7), ("ring_10", 4),
+    ("ring_9", 5), ("gradient", 4), ("ring_10", 3), ("xf_7", 6), ("gradient", 3), ("two_6", 7),
     ("ring_10", 5), ("gradient", 6), ("gradient", 7), ("gradient", 5),
 )
 LAST_OWN, LAST_OTHER = 5, 5

time: 86.9 us -> 87.3 us (level)
  no operation moved by 1% of the time
where the time goes in v5:
time: 87.3 us; the launch traced here: 87.2 us
  Pallas kernels  86.4 us (99%)
    pallas_call x1, Pallas kernels, on_device(): pl.pallas_call(kernel, out_shape=(pltpu.VMEM((FULL, DEPTH), jnp.float32),...  83.9 us
    pallas_call x1, Pallas kernels, on_device(): pl.pallas_call(finish, out_shape=(jax.ShapeDtypeStruct((FULL, DEPTH), jnp...  2.49 us

profile of v5, /device:TPU:1, one launch (start us, length us, event | category | flops | bytes accessed | tf_op | source)
XLA Modules:
  0.0 87.2 jit_solution(5014405981665422444)
XLA Ops:
  0.6 83.9 %shard_map.50 = (f32[1024,1280]{1,0:T(8,128)S(1)}, f32[64,1024]{1,0:T(8,128)S(1)}) custom-call(bf16[1024,1280]{1,0:T(8,128)(2,1)} %r_hbm.1, bf16[1280,256]{1,0:T(8,128)(2,1)} %s_hbm.1, f32[64,1024]{1,0:T(8,128)} %c_hbm.1), custom_call_target="tpu_custom_call" | custom-call | flops 10737418240 | bytes 9437184 | tf_op jit(solution)/shard_map/pallas_call | solution.py:545
  84.5 2.5 %shard_map.51 = (f32[1024,1280]{1,0:T(8,128)}, f32[64,1024]{1,0:T(8,128)}) custom-call(f32[1024,1280]{1,0:T(8,128)S(1)} %get-tuple-element.4.g_ref, f32[64,1024]{1,0:T(8,128)S(1)} %get-tuple-element.5.res_ref), custom_call_target="tpu_custom_call" | custom-call | tf_op jit(solution)/shard_map/pallas_call | solution.py:586

commit v6 on v5

--- a/solution.py
+++ b/solution.py
@@ -38,7 +38,7 @@
     ("ring_9", 5), ("gradient", 4), ("ring_10", 3), ("xf_7", 6), ("gradient", 3), ("two_6", 7),
     ("ring_10", 5), ("gradient", 6), ("gradient", 7), ("gradient", 5),
 )
-LAST_OWN, LAST_OTHER = 5, 5
+OWN_ENDS, OTHER_ENDS = (0, 5), (0, 5)
 
 
 def code(v):
@@ -47,9 +47,9 @@
 
 def decode(b):
     b = b.astype(jnp.float32)
-    m = jnp.maximum(jnp.abs(b), 1e-36)
-    m = m * lax.rsqrt(m)
-    m = m * lax.rsqrt(m)
+    m = jnp.abs(b)
+    m = m * lax.rsqrt(jnp.maximum(m, 1e-36))
+    m = m * lax.rsqrt(jnp.maximum(m, 1e-18))
     return jnp.where(b < 0, -m, m)
 
 
@@ -140,7 +140,6 @@
 
     c_in.wait()
     cmd_t[...] = cpad[...].T
-    g_ref[...] = jnp.zeros_like(g_ref)
     r_in.wait()
 
     own0 = core * HALF
@@ -198,17 +197,19 @@
 
     scale_factor = 1.0 / jnp.sqrt(jnp.float32(2048))
 
-    def add_gradient(g, start, last):
+    def add_gradient(g, start, ends):
         here = rows(start, HALF)
-        added = g_ref[here, :] + lax.dot_general(
+        added = lax.dot_general(
             rall[g, here, :], sall[g], (((1,), (1,)), ((), ())),
             preferred_element_type=jnp.float32,
         )
-        g_ref[here, :] = added * scale_factor if g == last else added
+        if g != ends[0]:
+            added = g_ref[here, :] + added
+        g_ref[here, :] = added * scale_factor if g == ends[1] else added
 
     def share(g):
         out_core(g).start()
-        add_gradient(g, own0, LAST_OWN)
+        add_gradient(g, own0, OWN_ENDS)
 
     def with_twin(g, here):
         return acc[g, here, :] + decode(crecv[g, here, :])
@@ -485,7 +486,7 @@
 
     def stage_gradient(g):
         in_core(g).wait_recv()
-        add_gradient(g, other0, LAST_OTHER)
+        add_gradient(g, other0, OTHER_ENDS)
 
         @pl.when(g == my_slot)
         def _():

time: 87.3 us -> 87.3 us (level)
  no operation moved by 1% of the time
where the time goes in v6:
time: 87.3 us; the launch traced here: 87.2 us
  Pallas kernels  86.3 us (99%)
    pallas_call x1, Pallas kernels, on_device(): pl.pallas_call(kernel, out_shape=(pltpu.VMEM((FULL, DEPTH), jnp.float32),...  83.9 us
    pallas_call x1, Pallas kernels, on_device(): pl.pallas_call(finish, out_shape=(jax.ShapeDtypeStruct((FULL, DEPTH), jnp...  2.49 us

profile of v6, /device:TPU:1, one launch (start us, length us, event | category | flops | bytes accessed | tf_op | source)
XLA Modules:
  0.0 87.2 jit_solution(10516349300112735435)
XLA Ops:
  0.6 83.9 %shard_map.50 = (f32[1024,1280]{1,0:T(8,128)S(1)}, f32[64,1024]{1,0:T(8,128)S(1)}) custom-call(bf16[1024,1280]{1,0:T(8,128)(2,1)} %r_hbm.1, bf16[1280,256]{1,0:T(8,128)(2,1)} %s_hbm.1, f32[64,1024]{1,0:T(8,128)} %c_hbm.1), custom_call_target="tpu_custom_call" | custom-call | flops 10737418240 | bytes 9437184 | tf_op jit(solution)/shard_map/pallas_call | solution.py:546
  84.5 2.5 %shard_map.51 = (f32[1024,1280]{1,0:T(8,128)}, f32[64,1024]{1,0:T(8,128)}) custom-call(f32[1024,1280]{1,0:T(8,128)S(1)} %get-tuple-element.4.g_ref, f32[64,1024]{1,0:T(8,128)S(1)} %get-tuple-element.5.res_ref), custom_call_target="tpu_custom_call" | custom-call | tf_op jit(solution)/shard_map/pallas_call | solution.py:587

commit v7 on v4

--- a/solution.py
+++ b/solution.py
@@ -38,7 +38,7 @@
     ("ring_10", 3), ("ring_9", 5), ("gradient", 4), ("gradient", 3), ("xf_7", 6), ("two_6", 7),
     ("ring_10", 5), ("gradient", 6), ("gradient", 7), ("gradient", 5),
 )
-LAST_OWN, LAST_OTHER = 5, 5
+OWN_ENDS, OTHER_ENDS = (0, 5), (1, 5)
 
 
 def code(v):
@@ -47,9 +47,9 @@
 
 def decode(b):
     b = b.astype(jnp.float32)
-    m = jnp.maximum(jnp.abs(b), 1e-36)
-    m = m * lax.rsqrt(m)
-    m = m * lax.rsqrt(m)
+    m = jnp.abs(b)
+    m = m * lax.rsqrt(jnp.maximum(m, 1e-36))
+    m = m * lax.rsqrt(jnp.maximum(m, 1e-18))
     return jnp.where(b < 0, -m, m)
 
 
@@ -140,7 +140,6 @@
 
     c_in.wait()
     cmd_t[...] = cpad[...].T
-    g_ref[...] = jnp.zeros_like(g_ref)
     r_in.wait()
 
     own0 = core * HALF
@@ -198,17 +197,19 @@
 
     scale_factor = 1.0 / jnp.sqrt(jnp.float32(2048))
 
-    def add_gradient(g, start, last):
+    def add_gradient(g, start, ends):
         here = rows(start, HALF)
-        added = g_ref[here, :] + lax.dot_general(
+        added = lax.dot_general(
             rall[g, here, :], sall[g], (((1,), (1,)), ((), ())),
             preferred_element_type=jnp.float32,
         )
-        g_ref[here, :] = added * scale_factor if g == last else added
+        if g != ends[0]:
+            added = g_ref[here, :] + added
+        g_ref[here, :] = added * scale_factor if g == ends[1] else added
 
     def share(g):
         out_core(g).start()
-        add_gradient(g, own0, LAST_OWN)
+        add_gradient(g, own0, OWN_ENDS)
 
     def with_twin(g, here):
         return acc[g, here, :] + decode(crecv[g, here, :])
@@ -485,7 +486,7 @@
 
     def stage_gradient(g):
         in_core(g).wait_recv()
-        add_gradient(g, other0, LAST_OTHER)
+        add_gradient(g, other0, OTHER_ENDS)
 
         @pl.when(g == my_slot)
         def _():

time: 86.9 us -> 86.9 us (level)
  no operation moved by 1% of the time
where the time goes in v7:
time: 86.9 us
  Pallas kernels  86 us (99%)
    pallas_call x1, Pallas kernels, on_device(): pl.pallas_call(kernel, out_shape=(pltpu.VMEM((FULL, DEPTH), jnp.float32),...  83.5 us
    pallas_call x1, Pallas kernels, on_device(): pl.pallas_call(finish, out_shape=(jax.ShapeDtypeStruct((FULL, DEPTH), jnp...  2.49 us

profile of v7, /device:TPU:1, one launch (start us, length us, event | category | flops | bytes accessed | tf_op | source)
XLA Modules:
  0.0 86.9 jit_solution(5772837703149880155)
XLA Ops:
  0.6 83.5 %shard_map.50 = (f32[1024,1280]{1,0:T(8,128)S(1)}, f32[64,1024]{1,0:T(8,128)S(1)}) custom-call(bf16[1024,1280]{1,0:T(8,128)(2,1)} %r_hbm.1, bf16[1280,256]{1,0:T(8,128)(2,1)} %s_hbm.1, f32[64,1024]{1,0:T(8,128)} %c_hbm.1), custom_call_target="tpu_custom_call" | custom-call | flops 10737418240 | bytes 9437184 | tf_op jit(solution)/shard_map/pallas_call | solution.py:546
  84.2 2.5 %shard_map.51 = (f32[1024,1280]{1,0:T(8,128)}, f32[64,1024]{1,0:T(8,128)}) custom-call(f32[1024,1280]{1,0:T(8,128)S(1)} %get-tuple-element.4.g_ref, f32[64,1024]{1,0:T(8,128)S(1)} %get-tuple-element.5.res_ref), custom_call_target="tpu_custom_call" | custom-call | tf_op jit(solution)/shard_map/pallas_call | solution.py:587
